TPU v7x, 32 devices: a whole 2x2x4 slice. The times are simulated.
32 devices in a mesh: inst: 4 (over y, x), cell: 8 (over z, core).
Axes of the slice: x: 2, y: 2, z: 4, core: 2. Of those that a mesh axis runs over, the one named last changes fastest.
Arguments:
- adjoint_init: float32 [8, 24, 8, 320], P('inst', 'cell'), may hold values from -6 to 6
- source_term: float32 [8, 24, 8, 320], P('inst', 'cell'), may hold values from -6 to 6
- jacobian: bfloat16 [8, 24, 3, 320, 320], P('inst', 'cell')
- volume: float32 [24, 320], P('cell'), may hold values from 0.5 to 2
- pseudo_step: float32 [24, 320], P('cell'), may hold values from 0.2 to 0.6
- neighbor_slots: int32 [24, 3], P('cell'), may hold values from 0 to 6, as said below
- halo_blocks: int32 [32], P('cell'), may hold values from 0 to 2, as said below
- padded_rows: int32 [8], P('cell'), may hold values from 0 to 1
Outputs:
- adjoint: float32 [8, 24, 8, 320], P('inst', 'cell')
- residual: float32 [8, 24, 8, 320], P('inst', 'cell')
Inputs may be any that keep to these rules, and one draw needn't show every extreme that they name: `neighbor_slots`: slot 0 of block row r is its own block, 2 + (r mod 3); slot 1 is below 2; slot 2 is 5 or more. `halo_blocks`: each device's 2 * 2 entries are its local block rows, the first 2 for the previous device, the others for the next; every entry is below 3 minus that device's padded rows.
All inputs are finite; a program needn't handle non-finite values.
Results may differ from a plain program's by a relative error of at most 0.0003.
Values sent between devices are 32-bit elements; how exact they have to be, the bound alone decides.
A program may use at most 64 MiB of HBM per device.

v0:
```python
import functools
import math

import jax
import jax.numpy as jnp
from jax import lax
from jax.experimental import pallas as pl
from jax.experimental.pallas import tpu as pltpu
from jax.sharding import PartitionSpec as P

ITERS = 16
TERMS = 2
MESH = pl.DeviceIdType.MESH

spectral_scale = 0.15


def time_weight(diff, count):
    diff = diff % count
    if diff == 0:
        return 0.0
    angle = math.pi * diff / count
    return 0.5 * (-1.0) ** diff * math.cos(angle) / math.sin(angle)


def kernel(
    insts,
    cells,
    slots_ref,
    halo_ref,
    pad_ref,
    init_ref,
    src_in_ref,
    jac_ref,
    vol_ref,
    step_in_ref,
    adj_out,
    res_out,
    adj,
    halo_out,
    from_prev,
    from_next,
    peers,
    src,
    step,
    scale,
    near,
    far,
    prev_parts,
    next_parts,
    flux,
    send_sem,
    prev_sem,
    next_sem,
    peer_sem,
):
    rows, width = vol_ref.shape
    reach = from_prev.shape[1]
    objectives = adj.shape[2]
    packed = adj.shape[3]
    main = width // 128 * 128
    tail = width - main
    wide = main + 128
    a = lax.axis_index("inst")
    d = lax.axis_index("cell")
    before = lax.rem(d + cells - 1, cells)
    after = lax.rem(d + 1, cells)
    others = [lax.rem(a + m, insts) for m in range(1, insts)]

    barrier = pltpu.get_barrier_semaphore()
    for c in (before, after):
        pl.semaphore_signal(barrier, inc=1, device_id={"cell": c}, device_id_type=MESH)
    for b in others:
        pl.semaphore_signal(barrier, inc=1, device_id={"inst": b}, device_id_type=MESH)

    def pack(first, second):
        return jnp.concatenate(
            [first[:, :main], first[:, main:], second[:, main:], second[:, :main]], axis=1
        )

    for r in range(rows):
        adj[0, r] = pack(init_ref[0, r], init_ref[1, r])
        src[r] = pack(src_in_ref[0, r], src_in_ref[1, r])
        v = jnp.broadcast_to(vol_ref[r : r + 1, :], (objectives, width)) * spectral_scale
        scale[r] = pack(v, v)
        v = jnp.broadcast_to(step_in_ref[r : r + 1, :], (objectives, width))
        step[r] = pack(v, v)

    def expand(t, r, k, dst):
        block = jac_ref.at[t, r, k]
        if t == 0:
            dst[:width, :main] = block[:, :main]
            dst[:width, main:] = jnp.concatenate(
                [block[:, main:], jnp.zeros((width, 128 - tail), jnp.bfloat16)], axis=1
            )
            dst[width:, :] = jnp.zeros((wide - width, wide), jnp.bfloat16)
        else:
            for lo, hi, at in ((0, main, 128), (main, width, 128 - tail)):
                dst[at : at + hi - lo, 128:] = block[lo:hi, :main]
                dst[at : at + hi - lo, :128] = jnp.concatenate(
                    [jnp.zeros((hi - lo, 128 - tail), jnp.bfloat16), block[lo:hi, main:]], axis=1
                )
            dst[: 128 - tail, :] = jnp.zeros((128 - tail, wide), jnp.bfloat16)

    for r in range(rows):
        for t in range(2):
            expand(t, r, 0, near.at[r, t])
            for k in (1, 2):
                expand(t, r, k, far.at[r, t, (k - 1) * wide : k * wide, :])

    def split(x):
        parts = []
        for _ in range(TERMS):
            high = x.astype(jnp.bfloat16).astype(jnp.float32)
            parts.append(high)
            x = x - high
        return jnp.concatenate(parts, axis=0).astype(jnp.bfloat16)

    def join(x):
        total = x[objectives * (TERMS - 1) :]
        for n in reversed(range(TERMS - 1)):
            total = total + x[objectives * n : objectives * (n + 1)]
        return total

    def merge(first, second):
        return jnp.concatenate(
            [first[:, :main], first[:, main:] + second[:, :128], second[:, 128:]], axis=1
        )

    live = [
        jnp.where(r < rows - pad_ref[0], jnp.float32(1), jnp.float32(0)) for r in range(rows)
    ]
    lane = lax.broadcasted_iota(jnp.int32, (objectives, 128), 1)
    first_half = lane < tail

    pl.semaphore_wait(barrier, insts + 1)

    def sweep(s, carry):
        now = lax.rem(s, 2)
        later = 1 - now
        for h in range(2 * reach):
            halo_out[now, h] = adj[now, halo_ref[h]]
        copies = [
            pltpu.make_async_remote_copy(
                halo_out.at[now, 0:reach],
                from_next.at[now],
                send_sem.at[now, 0],
                next_sem.at[now],
                device_id={"cell": before},
                device_id_type=MESH,
            ),
            pltpu.make_async_remote_copy(
                halo_out.at[now, reach : 2 * reach],
                from_prev.at[now],
                send_sem.at[now, 1],
                prev_sem.at[now],
                device_id={"cell": after},
                device_id_type=MESH,
            ),
        ]
        for m in range(1, insts):
            copies.append(
                pltpu.make_async_remote_copy(
                    adj.at[now],
                    peers.at[now, insts - m - 1],
                    send_sem.at[now, 1 + m],
                    peer_sem.at[now, insts - m - 1],
                    device_id={"inst": others[m - 1]},
                    device_id_type=MESH,
                )
            )
        for copy in copies:
            copy.start()

        for r in range(rows):
            x = split(adj[now, r])
            flux[r] = merge(
                join(jnp.dot(x[:, :wide], near[r, 0], preferred_element_type=jnp.float32)),
                join(jnp.dot(x[:, packed - wide :], near[r, 1], preferred_element_type=jnp.float32)),
            )

        copies[0].wait_recv()
        for h in range(reach):
            next_parts[h] = split(from_next[now, h])
        copies[1].wait_recv()
        for h in range(reach):
            prev_parts[h] = split(from_prev[now, h])
        for r in range(rows):
            p = prev_parts[jnp.clip(slots_ref[r, 1], 0, reach - 1)]
            q = next_parts[jnp.clip(slots_ref[r, 2] - reach - rows, 0, reach - 1)]
            flux[r] += merge(
                join(
                    jnp.dot(
                        jnp.concatenate([p[:, :wide], q[:, :wide]], axis=1),
                        far[r, 0],
                        preferred_element_type=jnp.float32,
                    )
                ),
                join(
                    jnp.dot(
                        jnp.concatenate([p[:, packed - wide :], q[:, packed - wide :]], axis=1),
                        far[r, 1],
                        preferred_element_type=jnp.float32,
                    )
                ),
            )

        for copy in copies[2:]:
            copy.wait_recv()
        count = 2 * insts
        for r in range(rows):
            first, middle, second = 0.0, 0.0, 0.0
            cross = 0.0
            for m in range(insts):
                u = adj[now, r] if m == 0 else peers[now, m - 1, r]
                same = time_weight(2 * m, count)
                up = time_weight(2 * m + 1, count)
                down = time_weight(2 * m - 1, count)
                u0, ut, u1 = u[:, :main], u[:, main:wide], u[:, wide:]
                first = first + same * u0 + up * u1
                second = second + same * u1 + down * u0
                middle = middle + same * ut
                cross = cross + jnp.where(first_half, down, up) * ut
            middle = middle + pltpu.roll(cross, tail, 1)
            coupled = jnp.concatenate([first, middle, second], axis=1)
            old = adj[now, r]
            residual = live[r] * (src[r] - flux[r] - scale[r] * coupled)
            new = old + step[r] * residual
            adj[later, r] = new

            @pl.when(s == ITERS - 1)
            def _():
                for out, value in ((adj_out, new), (res_out, residual)):
                    out[0, r, :, :main] = value[:, :main]
                    out[0, r, :, main:] = value[:, main:width]
                    out[1, r, :, :main] = value[:, wide:]
                    out[1, r, :, main:] = value[:, width:wide]

        for copy in copies:
            copy.wait_send()
        return carry

    lax.fori_loop(0, ITERS, sweep, 0)


def on_device(
    insts,
    cells,
    adjoint_init,
    source_term,
    jacobian,
    volume,
    pseudo_step,
    neighbor_slots,
    halo_blocks,
    padded_rows,
):
    inst_local, rows, objectives, width = adjoint_init.shape
    reach = halo_blocks.shape[0] // 2
    main = width // 128 * 128
    wide = main + 128
    packed = inst_local * width
    out = jax.ShapeDtypeStruct(adjoint_init.shape, jnp.float32)
    smem = pl.BlockSpec(memory_space=pltpu.SMEM)
    vmem = pl.BlockSpec(memory_space=pltpu.VMEM)
    f32, bf16 = jnp.float32, jnp.bfloat16
    block = (objectives, packed)
    parts = (objectives * TERMS, packed)
    flops = ITERS * 2 * rows * 3 * inst_local * 16 * width * width
    return pl.pallas_call(
        functools.partial(kernel, insts, cells),
        out_shape=(out, out),
        in_specs=[smem] * 3 + [vmem] * 5,
        out_specs=(vmem, vmem),
        scratch_shapes=[
            pltpu.VMEM((2, rows) + block, f32),
            pltpu.VMEM((2, 2 * reach) + block, f32),
            pltpu.VMEM((2, reach) + block, f32),
            pltpu.VMEM((2, reach) + block, f32),
            pltpu.VMEM((2, insts - 1, rows) + block, f32),
            pltpu.VMEM((rows,) + block, f32),
            pltpu.VMEM((rows,) + block, f32),
            pltpu.VMEM((rows,) + block, f32),
            pltpu.VMEM((rows, 2, wide, wide), bf16),
            pltpu.VMEM((rows, 2, 2 * wide, wide), bf16),
            pltpu.VMEM((reach,) + parts, bf16),
            pltpu.VMEM((reach,) + parts, bf16),
            pltpu.VMEM((rows,) + block, f32),
            pltpu.SemaphoreType.DMA((2, insts + 1)),
            pltpu.SemaphoreType.DMA((2,)),
            pltpu.SemaphoreType.DMA((2,)),
            pltpu.SemaphoreType.DMA((2, insts - 1)),
        ],
        compiler_params=pltpu.CompilerParams(
            collective_id=0, has_side_effects=True, vmem_limit_bytes=40 * 1024 * 1024
        ),
        cost_estimate=pl.CostEstimate(
            flops=flops, bytes_accessed=2 * jacobian.size, transcendentals=0
        ),
        name="relax",
    )(
        neighbor_slots,
        halo_blocks,
        padded_rows,
        adjoint_init,
        source_term,
        jacobian,
        volume,
        pseudo_step,
    )


def solution(mesh):
    return jax.shard_map(
        functools.partial(on_device, mesh.shape["inst"], mesh.shape["cell"]),
        mesh=mesh,
        in_specs=(
            P("inst", "cell", None, None),
            P("inst", "cell", None, None),
            P("inst", "cell", None, None, None),
            P("cell", None),
            P("cell", None),
            P("cell", None),
            P("cell"),
            P("cell"),
        ),
        out_specs=(P("inst", "cell", None, None), P("inst", "cell", None, None)),
        check_vma=False,
    )
```

profile of v0, /device:TPU:0, one launch (start us, length us, event | category | flops | bytes accessed | tf_op | source)
XLA Modules:
  0.0 88.9 jit_solution(7423776742277025268)
XLA Ops:
  1.3 0.0 copy-start
  1.3 2.2 %copy-done = bf16[2,3,3,320,320]{4,3,2,1,0:T(8,128)(2,1)S(1)} copy-done((bf16[2,3,3,320,320]{4,3,2,1,0:T(8,128)(2,1)S(1)}, bf16[2,3,3,320,320]{4,3,2,1,0:T(8,128)(2,1)}, u32[]{:S(2)}) %copy-start) | copy-done | bytes 3686424
  3.5 0.0 copy-start.1
  3.5 0.9 copy-done.1
  4.4 0.0 copy-start.2
  4.4 0.9 copy-done.2
  5.3 0.0 copy-start.3
  5.3 0.7 copy-done.3
  6.0 0.0 copy-start.4
  6.0 0.7 copy-done.4
  6.7 0.0 copy-start.5
  6.7 0.7 copy-done.5
  7.4 0.0 copy-start.6
  7.4 0.7 copy-done.6
  8.0 79.6 %relax.1 = (f32[2,3,8,320]{3,2,1,0:T(8,128)S(1)}, f32[2,3,8,320]{3,2,1,0:T(8,128)S(1)}) custom-call(s32[3,3]{1,0:T(4,128)S(1)} %copy-done.5, s32[4]{0:T(128)S(1)} %copy-done.6, s32[1]{0:T(128)S(6)} %copy.12.pad_ref, f32[2,3,8,320]{3,2,1,0:T(8,128)S(1)} %copy-done.1, f32[2,3,8,320]{3,2,1,0:T(8,128)S(1)} %copy-done.2, ...), custom_call_target="tpu_custom_call" | custom-call | flops 943718400 | bytes 3686400 | tf_op jit(solution)/shard_map/relax/pallas_call | solution.py:270
  87.6 0.6 copy.13
  88.2 0.6 copy.14
Async XLA Ops:
  1.3 2.3 %copy-start = (bf16[2,3,3,320,320]{4,3,2,1,0:T(8,128)(2,1)S(1)}, bf16[2,3,3,320,320]{4,3,2,1,0:T(8,128)(2,1)}, u32[]{:S(2)}) copy-start(bf16[2,3,3,320,320]{4,3,2,1,0:T(8,128)(2,1)} %jac_ref.1) | copy-start | bytes 11059204
  3.5 0.9 copy-start.1
  4.4 0.9 copy-start.2
  5.3 0.7 copy-start.3
  6.0 0.7 copy-start.4
  6.7 0.7 copy-start.5
  7.4 0.7 copy-start.6
where the time goes:
time: 89.2 us; the launch traced here: 88.9 us
  Pallas kernels  79.6 us (89%)
  local copies, waits for them, and re-layouts  8 us (9%)
  between operations  1.3 us (1%)
    pallas_call x1, Pallas kernels, on_device(): pl.pallas_call(functools.partial(kernel, insts, cells), out_shape=(out, o...  79.6 us
    unnamed x16, local copies, waits for them, and re-layouts  8 us

commit v1 on v0

--- a/solution.py
+++ b/solution.py
@@ -29,18 +29,25 @@
     slots_ref,
     halo_ref,
     pad_ref,
+    init_hbm,
+    src_hbm,
+    jac_hbm,
+    vol_hbm,
+    step_hbm,
+    adj_out,
+    res_out,
     init_ref,
     src_in_ref,
     jac_ref,
     vol_ref,
     step_in_ref,
-    adj_out,
-    res_out,
     adj,
     halo_out,
     from_prev,
     from_next,
-    peers,
+    raw_in,
+    part_out,
+    part_in,
     src,
     step,
     scale,
@@ -49,12 +56,16 @@
     prev_parts,
     next_parts,
     flux,
+    coupled,
     send_sem,
     prev_sem,
     next_sem,
-    peer_sem,
+    raw_sem,
+    part_sem,
+    load_sem,
 ):
     rows, width = vol_ref.shape
+    assert insts == 4
     reach = from_prev.shape[1]
     objectives = adj.shape[2]
     packed = adj.shape[3]
@@ -65,12 +76,36 @@
     d = lax.axis_index("cell")
     before = lax.rem(d + cells - 1, cells)
     after = lax.rem(d + 1, cells)
-    others = [lax.rem(a + m, insts) for m in range(1, insts)]
+    x_odd = lax.rem(a, 2)
+    even = x_odd == 0
+    x_peer = a + 1 - 2 * x_odd
+    y_peer = lax.rem(a + 2, insts)
+    cut = (rows + 1) // 2
+    swap = lax.rem(d, 2)
+    near_x = swap == 0
+    one = x_peer + swap * (y_peer - x_peer)
+    two = y_peer + swap * (x_peer - y_peer)
+    groups = [(slice(0, cut), one, two, near_x), (slice(cut, rows), two, one, swap == 1)]
+
+    loads = [
+        pltpu.make_async_copy(hbm, ref, load_sem.at[n])
+        for n, (hbm, ref) in enumerate(
+            (
+                (init_hbm, init_ref),
+                (src_hbm, src_in_ref),
+                (vol_hbm, vol_ref),
+                (step_hbm, step_in_ref),
+                (jac_hbm, jac_ref),
+            )
+        )
+    ]
+    for load in loads:
+        load.start()
 
     barrier = pltpu.get_barrier_semaphore()
     for c in (before, after):
         pl.semaphore_signal(barrier, inc=1, device_id={"cell": c}, device_id_type=MESH)
-    for b in others:
+    for b in (x_peer, y_peer):
         pl.semaphore_signal(barrier, inc=1, device_id={"inst": b}, device_id_type=MESH)
 
     def pack(first, second):
@@ -78,6 +113,8 @@
             [first[:, :main], first[:, main:], second[:, main:], second[:, :main]], axis=1
         )
 
+    for load in loads[:4]:
+        load.wait()
     for r in range(rows):
         adj[0, r] = pack(init_ref[0, r], init_ref[1, r])
         src[r] = pack(src_in_ref[0, r], src_in_ref[1, r])
@@ -102,12 +139,6 @@
                 )
             dst[: 128 - tail, :] = jnp.zeros((128 - tail, wide), jnp.bfloat16)
 
-    for r in range(rows):
-        for t in range(2):
-            expand(t, r, 0, near.at[r, t])
-            for k in (1, 2):
-                expand(t, r, k, far.at[r, t, (k - 1) * wide : k * wide, :])
-
     def split(x):
         parts = []
         for _ in range(TERMS):
@@ -133,7 +164,29 @@
     lane = lax.broadcasted_iota(jnp.int32, (objectives, 128), 1)
     first_half = lane < tail
 
-    pl.semaphore_wait(barrier, insts + 1)
+    pl.semaphore_wait(barrier, 4)
+
+    count = 2 * insts
+
+    def weights(offset):
+        return [time_weight(2 * offset + n, count) for n in (0, 1, -1)]
+
+    def choose(flag, first, second):
+        return [jnp.where(flag, jnp.float32(p), jnp.float32(q)) for p, q in zip(first, second)]
+
+    ahead = choose(even, weights(1), weights(-1))
+    behind = choose(even, weights(-1), weights(1))
+    across = weights(2)
+
+    def mix(sources):
+        first, middle, second, cross = 0.0, 0.0, 0.0, 0.0
+        for u, (same, up, down) in sources:
+            u0, ut, u1 = u[:, :main], u[:, main:wide], u[:, wide:]
+            first = first + same * u0 + up * u1
+            second = second + same * u1 + down * u0
+            middle = middle + same * ut
+            cross = cross + jnp.where(first_half, down, up) * ut
+        return jnp.concatenate([first, middle + pltpu.roll(cross, tail, 1), second], axis=1)
 
     def sweep(s, carry):
         now = lax.rem(s, 2)
@@ -158,19 +211,28 @@
                 device_id_type=MESH,
             ),
         ]
-        for m in range(1, insts):
+        for g, (part, to, _, _) in enumerate(groups):
             copies.append(
                 pltpu.make_async_remote_copy(
-                    adj.at[now],
-                    peers.at[now, insts - m - 1],
-                    send_sem.at[now, 1 + m],
-                    peer_sem.at[now, insts - m - 1],
-                    device_id={"inst": others[m - 1]},
+                    adj.at[now, part],
+                    raw_in.at[now, part],
+                    send_sem.at[now, 2 + g],
+                    raw_sem.at[now, g],
+                    device_id={"inst": to},
                     device_id_type=MESH,
                 )
             )
         for copy in copies:
             copy.start()
+
+        @pl.when(s == 0)
+        def _():
+            loads[4].wait()
+            for r in range(rows):
+                for t in range(2):
+                    expand(t, r, 0, near.at[r, t])
+                    for k in (1, 2):
+                        expand(t, r, k, far.at[r, t, (k - 1) * wide : k * wide, :])
 
         for r in range(rows):
             x = split(adj[now, r])
@@ -178,6 +240,27 @@
                 join(jnp.dot(x[:, :wide], near[r, 0], preferred_element_type=jnp.float32)),
                 join(jnp.dot(x[:, packed - wide :], near[r, 1], preferred_element_type=jnp.float32)),
             )
+
+        for g, (part, _, to, x_first) in enumerate(groups):
+            copies[2 + g].wait_recv()
+            mine = choose(x_first, across, behind)
+            theirs = choose(x_first, behind, ahead)
+            for r in range(part.start, part.stop):
+                part_out[now, r] = mix([(adj[now, r], mine), (raw_in[now, r], theirs)])
+            copy = pltpu.make_async_remote_copy(
+                part_out.at[now, part],
+                part_in.at[now, part],
+                send_sem.at[now, 4 + g],
+                part_sem.at[now, g],
+                device_id={"inst": to},
+                device_id_type=MESH,
+            )
+            copy.start()
+            copies.append(copy)
+        for part, _, _, x_first in groups:
+            theirs = choose(x_first, ahead, across)
+            for r in range(part.start, part.stop):
+                coupled[r] = mix([(adj[now, r], weights(0)), (raw_in[now, r], theirs)])
 
         copies[0].wait_recv()
         for h in range(reach):
@@ -205,26 +288,11 @@
                 ),
             )
 
-        for copy in copies[2:]:
+        for copy in copies[4:]:
             copy.wait_recv()
-        count = 2 * insts
         for r in range(rows):
-            first, middle, second = 0.0, 0.0, 0.0
-            cross = 0.0
-            for m in range(insts):
-                u = adj[now, r] if m == 0 else peers[now, m - 1, r]
-                same = time_weight(2 * m, count)
-                up = time_weight(2 * m + 1, count)
-                down = time_weight(2 * m - 1, count)
-                u0, ut, u1 = u[:, :main], u[:, main:wide], u[:, wide:]
-                first = first + same * u0 + up * u1
-                second = second + same * u1 + down * u0
-                middle = middle + same * ut
-                cross = cross + jnp.where(first_half, down, up) * ut
-            middle = middle + pltpu.roll(cross, tail, 1)
-            coupled = jnp.concatenate([first, middle, second], axis=1)
             old = adj[now, r]
-            residual = live[r] * (src[r] - flux[r] - scale[r] * coupled)
+            residual = live[r] * (src[r] - flux[r] - scale[r] * (coupled[r] + part_in[now, r]))
             new = old + step[r] * residual
             adj[later, r] = new
 
@@ -270,14 +338,21 @@
     return pl.pallas_call(
         functools.partial(kernel, insts, cells),
         out_shape=(out, out),
-        in_specs=[smem] * 3 + [vmem] * 5,
+        in_specs=[smem] * 3 + [pl.BlockSpec(memory_space=pltpu.HBM)] * 5,
         out_specs=(vmem, vmem),
         scratch_shapes=[
+            pltpu.VMEM(adjoint_init.shape, f32),
+            pltpu.VMEM(adjoint_init.shape, f32),
+            pltpu.VMEM(jacobian.shape, bf16),
+            pltpu.VMEM(volume.shape, f32),
+            pltpu.VMEM(volume.shape, f32),
             pltpu.VMEM((2, rows) + block, f32),
             pltpu.VMEM((2, 2 * reach) + block, f32),
             pltpu.VMEM((2, reach) + block, f32),
             pltpu.VMEM((2, reach) + block, f32),
-            pltpu.VMEM((2, insts - 1, rows) + block, f32),
+            pltpu.VMEM((2, rows) + block, f32),
+            pltpu.VMEM((2, rows) + block, f32),
+            pltpu.VMEM((2, rows) + block, f32),
             pltpu.VMEM((rows,) + block, f32),
             pltpu.VMEM((rows,) + block, f32),
             pltpu.VMEM((rows,) + block, f32),
@@ -286,10 +361,13 @@
             pltpu.VMEM((reach,) + parts, bf16),
             pltpu.VMEM((reach,) + parts, bf16),
             pltpu.VMEM((rows,) + block, f32),
-            pltpu.SemaphoreType.DMA((2, insts + 1)),
+            pltpu.VMEM((rows,) + block, f32),
+            pltpu.SemaphoreType.DMA((2, 6)),
             pltpu.SemaphoreType.DMA((2,)),
             pltpu.SemaphoreType.DMA((2,)),
-            pltpu.SemaphoreType.DMA((2, insts - 1)),
+            pltpu.SemaphoreType.DMA((2, 2)),
+            pltpu.SemaphoreType.DMA((2, 2)),
+            pltpu.SemaphoreType.DMA((5,)),
         ],
         compiler_params=pltpu.CompilerParams(
             collective_id=0, has_side_effects=True, vmem_limit_bytes=40 * 1024 * 1024

time: 89.2 us -> 117 us (1.31)
  Pallas kernels: 79.6 us -> 108 us
    pallas_call x1, Pallas kernels: 79.6 us -> 108 us  [on_device(): pl.pallas_call(functools.partial(kernel, insts, cells), out_shape=(out, o...]
where the time goes in v1:
time: 117 us
  Pallas kernels  108 us (92%)
  local copies, waits for them, and re-layouts  8 us (7%)
  between operations  1.3 us (1%)
    pallas_call x1, Pallas kernels, on_device(): pl.pallas_call(functools.partial(kernel, insts, cells), out_shape=(out, o...  108 us
    unnamed x16, local copies, waits for them, and re-layouts  8 us

profile of v1, /device:TPU:0, one launch (start us, length us, event | category | flops | bytes accessed | tf_op | source)
XLA Modules:
  0.0 116.8 jit_solution(9928285403912428239)
XLA Ops:
  1.3 0.0 copy-start
  1.3 2.2 %copy-done = bf16[2,3,3,320,320]{4,3,2,1,0:T(8,128)(2,1)S(1)} copy-done((bf16[2,3,3,320,320]{4,3,2,1,0:T(8,128)(2,1)S(1)}, bf16[2,3,3,320,320]{4,3,2,1,0:T(8,128)(2,1)}, u32[]{:S(2)}) %copy-start) | copy-done | bytes 3686424
  3.5 0.0 copy-start.1
  3.5 0.9 copy-done.1
  4.4 0.0 copy-start.2
  4.4 0.9 copy-done.2
  5.3 0.0 copy-start.3
  5.3 0.7 copy-done.3
  6.0 0.0 copy-start.4
  6.0 0.7 copy-done.4
  6.7 0.0 copy-start.5
  6.7 0.7 copy-done.5
  7.4 0.0 copy-start.6
  7.4 0.7 copy-done.6
  8.0 107.5 %relax.1 = (f32[2,3,8,320]{3,2,1,0:T(8,128)S(1)}, f32[2,3,8,320]{3,2,1,0:T(8,128)S(1)}) custom-call(s32[3,3]{1,0:T(4,128)S(1)} %copy-done.5, s32[4]{0:T(128)S(1)} %copy-done.6, s32[1]{0:T(128)S(6)} %copy.12.pad_ref, f32[2,3,8,320]{3,2,1,0:T(8,128)S(1)} %copy-done.1, f32[2,3,8,320]{3,2,1,0:T(8,128)S(1)} %copy-done.2, ...), custom_call_target="tpu_custom_call" | custom-call | flops 943718400 | bytes 3686400 | tf_op jit(solution)/shard_map/relax/pallas_call | solution.py:338
  115.6 0.6 copy.13
  116.2 0.6 copy.14
Async XLA Ops:
  1.3 2.3 %copy-start = (bf16[2,3,3,320,320]{4,3,2,1,0:T(8,128)(2,1)S(1)}, bf16[2,3,3,320,320]{4,3,2,1,0:T(8,128)(2,1)}, u32[]{:S(2)}) copy-start(bf16[2,3,3,320,320]{4,3,2,1,0:T(8,128)(2,1)} %jac_hbm.1) | copy-start | bytes 11059204
  3.5 0.9 copy-start.1
  4.4 0.9 copy-start.2
  5.3 0.7 copy-start.3
  6.0 0.7 copy-start.4
  6.7 0.7 copy-start.5
  7.4 0.7 copy-start.6

commit v2 on v0

--- a/solution.py
+++ b/solution.py
@@ -29,33 +29,36 @@
     slots_ref,
     halo_ref,
     pad_ref,
+    init_hbm,
+    src_hbm,
+    jac_hbm,
+    vol_hbm,
+    step_hbm,
+    adj_out,
+    res_out,
     init_ref,
     src_in_ref,
     jac_ref,
     vol_ref,
     step_in_ref,
-    adj_out,
-    res_out,
     adj,
     halo_out,
-    from_prev,
-    from_next,
+    halo_in,
     peers,
     src,
     step,
     scale,
     near,
     far,
-    prev_parts,
-    next_parts,
+    parts,
     flux,
     send_sem,
-    prev_sem,
-    next_sem,
+    halo_sem,
     peer_sem,
+    load_sem,
 ):
     rows, width = vol_ref.shape
-    reach = from_prev.shape[1]
+    reach = halo_in.shape[2]
     objectives = adj.shape[2]
     packed = adj.shape[3]
     main = width // 128 * 128
@@ -66,6 +69,24 @@
     before = lax.rem(d + cells - 1, cells)
     after = lax.rem(d + 1, cells)
     others = [lax.rem(a + m, insts) for m in range(1, insts)]
+    close = 1 - lax.rem(d, 2)
+    sides = [close, 1 - close]
+    neighbour = [before + side * (after - before) for side in sides]
+
+    loads = [
+        pltpu.make_async_copy(hbm, ref, load_sem.at[n])
+        for n, (hbm, ref) in enumerate(
+            (
+                (init_hbm, init_ref),
+                (src_hbm, src_in_ref),
+                (vol_hbm, vol_ref),
+                (step_hbm, step_in_ref),
+                (jac_hbm, jac_ref),
+            )
+        )
+    ]
+    for load in loads:
+        load.start()
 
     barrier = pltpu.get_barrier_semaphore()
     for c in (before, after):
@@ -78,6 +99,8 @@
             [first[:, :main], first[:, main:], second[:, main:], second[:, :main]], axis=1
         )
 
+    for load in loads[:4]:
+        load.wait()
     for r in range(rows):
         adj[0, r] = pack(init_ref[0, r], init_ref[1, r])
         src[r] = pack(src_in_ref[0, r], src_in_ref[1, r])
@@ -102,12 +125,6 @@
                 )
             dst[: 128 - tail, :] = jnp.zeros((128 - tail, wide), jnp.bfloat16)
 
-    for r in range(rows):
-        for t in range(2):
-            expand(t, r, 0, near.at[r, t])
-            for k in (1, 2):
-                expand(t, r, k, far.at[r, t, (k - 1) * wide : k * wide, :])
-
     def split(x):
         parts = []
         for _ in range(TERMS):
@@ -135,29 +152,34 @@
 
     pl.semaphore_wait(barrier, insts + 1)
 
-    def sweep(s, carry):
-        now = lax.rem(s, 2)
-        later = 1 - now
-        for h in range(2 * reach):
-            halo_out[now, h] = adj[now, halo_ref[h]]
-        copies = [
-            pltpu.make_async_remote_copy(
-                halo_out.at[now, 0:reach],
-                from_next.at[now],
-                send_sem.at[now, 0],
-                next_sem.at[now],
-                device_id={"cell": before},
-                device_id_type=MESH,
-            ),
-            pltpu.make_async_remote_copy(
-                halo_out.at[now, reach : 2 * reach],
-                from_prev.at[now],
-                send_sem.at[now, 1],
-                prev_sem.at[now],
-                device_id={"cell": after},
-                device_id_type=MESH,
-            ),
-        ]
+    count = 2 * insts
+
+    def weights(offset):
+        return [time_weight(2 * offset + n, count) for n in (0, 1, -1)]
+
+    def mix(sources):
+        first, middle, second, cross = 0.0, 0.0, 0.0, 0.0
+        for u, (same, up, down) in sources:
+            u0, ut, u1 = u[:, :main], u[:, main:wide], u[:, wide:]
+            first = first + same * u0 + up * u1
+            second = second + same * u1 + down * u0
+            middle = middle + same * ut
+            cross = cross + jnp.where(first_half, down, up) * ut
+        return jnp.concatenate([first, middle + pltpu.roll(cross, tail, 1), second], axis=1)
+
+    def exchange(now):
+        copies = []
+        for n in range(2):
+            copies.append(
+                pltpu.make_async_remote_copy(
+                    halo_out.at[now, sides[n]],
+                    halo_in.at[now, 1 - sides[n]],
+                    send_sem.at[now, n],
+                    halo_sem.at[now, 1 - sides[n]],
+                    device_id={"cell": neighbour[n]},
+                    device_id_type=MESH,
+                )
+            )
         for m in range(1, insts):
             copies.append(
                 pltpu.make_async_remote_copy(
@@ -169,8 +191,35 @@
                     device_id_type=MESH,
                 )
             )
-        for copy in copies:
-            copy.start()
+        return copies
+
+    def arrival(now, n):
+        return pltpu.make_async_remote_copy(
+            halo_out.at[now, sides[n]],
+            halo_in.at[now, sides[n]],
+            send_sem.at[now, n],
+            halo_sem.at[now, sides[n]],
+            device_id={"cell": neighbour[n]},
+            device_id_type=MESH,
+        )
+
+    def sweep(s, carry):
+        now = lax.rem(s, 2)
+        later = 1 - now
+        for h in range(2 * reach):
+            halo_out[now, h // reach, h % reach] = adj[now, halo_ref[h]]
+        copies = exchange(now)
+        for n in [1, 0] + [m for m in (3, 2, 4) if m <= insts] + list(range(5, insts + 1)):
+            copies[n].start()
+
+        @pl.when(s == 0)
+        def _():
+            loads[4].wait()
+            for r in range(rows):
+                for t in range(2):
+                    expand(t, r, 0, near.at[r, t])
+                    for k in (1, 2):
+                        expand(t, r, k, far.at[k - 1, r, t])
 
         for r in range(rows):
             x = split(adj[now, r])
@@ -179,52 +228,41 @@
                 join(jnp.dot(x[:, packed - wide :], near[r, 1], preferred_element_type=jnp.float32)),
             )
 
-        copies[0].wait_recv()
-        for h in range(reach):
-            next_parts[h] = split(from_next[now, h])
-        copies[1].wait_recv()
-        for h in range(reach):
-            prev_parts[h] = split(from_prev[now, h])
-        for r in range(rows):
-            p = prev_parts[jnp.clip(slots_ref[r, 1], 0, reach - 1)]
-            q = next_parts[jnp.clip(slots_ref[r, 2] - reach - rows, 0, reach - 1)]
-            flux[r] += merge(
-                join(
-                    jnp.dot(
-                        jnp.concatenate([p[:, :wide], q[:, :wide]], axis=1),
-                        far[r, 0],
-                        preferred_element_type=jnp.float32,
-                    )
-                ),
-                join(
-                    jnp.dot(
-                        jnp.concatenate([p[:, packed - wide :], q[:, packed - wide :]], axis=1),
-                        far[r, 1],
-                        preferred_element_type=jnp.float32,
-                    )
-                ),
-            )
-
+        @pl.when(s > 0)
+        def _():
+            for copy in exchange(later):
+                copy.wait_send()
+
+        def incoming(n):
+            side = sides[n]
+            arrival(now, n).wait_recv()
+            for h in range(reach):
+                parts[h] = split(halo_in[now, side, h])
+            for r in range(rows):
+                code = slots_ref[r, 1 + side] - side * (reach + rows)
+                x = parts[jnp.clip(code, 0, reach - 1)]
+                yield merge(
+                    join(jnp.dot(x[:, :wide], far[side, r, 0], preferred_element_type=jnp.float32)),
+                    join(
+                        jnp.dot(
+                            x[:, packed - wide :],
+                            far[side, r, 1],
+                            preferred_element_type=jnp.float32,
+                        )
+                    ),
+                )
+
+        for r, value in enumerate(incoming(0)):
+            flux[r] += value
         for copy in copies[2:]:
             copy.wait_recv()
-        count = 2 * insts
         for r in range(rows):
-            first, middle, second = 0.0, 0.0, 0.0
-            cross = 0.0
-            for m in range(insts):
-                u = adj[now, r] if m == 0 else peers[now, m - 1, r]
-                same = time_weight(2 * m, count)
-                up = time_weight(2 * m + 1, count)
-                down = time_weight(2 * m - 1, count)
-                u0, ut, u1 = u[:, :main], u[:, main:wide], u[:, wide:]
-                first = first + same * u0 + up * u1
-                second = second + same * u1 + down * u0
-                middle = middle + same * ut
-                cross = cross + jnp.where(first_half, down, up) * ut
-            middle = middle + pltpu.roll(cross, tail, 1)
-            coupled = jnp.concatenate([first, middle, second], axis=1)
+            around = [(adj[now, r], weights(0))]
+            around += [(peers[now, m - 1, r], weights(m)) for m in range(1, insts)]
+            flux[r] = src[r] - flux[r] - scale[r] * mix(around)
+        for r, value in enumerate(incoming(1)):
             old = adj[now, r]
-            residual = live[r] * (src[r] - flux[r] - scale[r] * coupled)
+            residual = live[r] * (flux[r] - value)
             new = old + step[r] * residual
             adj[later, r] = new
 
@@ -236,11 +274,11 @@
                     out[1, r, :, :main] = value[:, wide:]
                     out[1, r, :, main:] = value[:, width:wide]
 
-        for copy in copies:
-            copy.wait_send()
         return carry
 
     lax.fori_loop(0, ITERS, sweep, 0)
+    for copy in exchange((ITERS - 1) % 2):
+        copy.wait_send()
 
 
 def on_device(
@@ -270,26 +308,29 @@
     return pl.pallas_call(
         functools.partial(kernel, insts, cells),
         out_shape=(out, out),
-        in_specs=[smem] * 3 + [vmem] * 5,
+        in_specs=[smem] * 3 + [pl.BlockSpec(memory_space=pltpu.HBM)] * 5,
         out_specs=(vmem, vmem),
         scratch_shapes=[
+            pltpu.VMEM(adjoint_init.shape, f32),
+            pltpu.VMEM(adjoint_init.shape, f32),
+            pltpu.VMEM(jacobian.shape, bf16),
+            pltpu.VMEM(volume.shape, f32),
+            pltpu.VMEM(volume.shape, f32),
             pltpu.VMEM((2, rows) + block, f32),
-            pltpu.VMEM((2, 2 * reach) + block, f32),
-            pltpu.VMEM((2, reach) + block, f32),
-            pltpu.VMEM((2, reach) + block, f32),
+            pltpu.VMEM((2, 2, reach) + block, f32),
+            pltpu.VMEM((2, 2, reach) + block, f32),
             pltpu.VMEM((2, insts - 1, rows) + block, f32),
             pltpu.VMEM((rows,) + block, f32),
             pltpu.VMEM((rows,) + block, f32),
             pltpu.VMEM((rows,) + block, f32),
             pltpu.VMEM((rows, 2, wide, wide), bf16),
-            pltpu.VMEM((rows, 2, 2 * wide, wide), bf16),
-            pltpu.VMEM((reach,) + parts, bf16),
+            pltpu.VMEM((2, rows, 2, wide, wide), bf16),
             pltpu.VMEM((reach,) + parts, bf16),
             pltpu.VMEM((rows,) + block, f32),
             pltpu.SemaphoreType.DMA((2, insts + 1)),
-            pltpu.SemaphoreType.DMA((2,)),
-            pltpu.SemaphoreType.DMA((2,)),
+            pltpu.SemaphoreType.DMA((2, 2)),
             pltpu.SemaphoreType.DMA((2, insts - 1)),
+            pltpu.SemaphoreType.DMA((5,)),
         ],
         compiler_params=pltpu.CompilerParams(
             collective_id=0, has_side_effects=True, vmem_limit_bytes=40 * 1024 * 1024

time: 89.2 us -> 94 us (1.054)
  Pallas kernels: 79.6 us -> 84.3 us
    pallas_call x1, Pallas kernels: 79.6 us -> 84.3 us  [on_device(): pl.pallas_call(functools.partial(kernel, insts, cells), out_shape=(out, o...]
where the time goes in v2:
time: 94 us; the launch traced here: 93.6 us
  Pallas kernels  84.3 us (90%)
  local copies, waits for them, and re-layouts  8 us (9%)
  between operations  1.3 us (1%)
    pallas_call x1, Pallas kernels, on_device(): pl.pallas_call(functools.partial(kernel, insts, cells), out_shape=(out, o...  84.3 us
    unnamed x16, local copies, waits for them, and re-layouts  8 us

profile of v2, /device:TPU:0, one launch (start us, length us, event | category | flops | bytes accessed | tf_op | source)
XLA Modules:
  0.0 93.6 jit_solution(17601160328199203922)
XLA Ops:
  1.3 0.0 copy-start
  1.3 2.2 %copy-done = bf16[2,3,3,320,320]{4,3,2,1,0:T(8,128)(2,1)S(1)} copy-done((bf16[2,3,3,320,320]{4,3,2,1,0:T(8,128)(2,1)S(1)}, bf16[2,3,3,320,320]{4,3,2,1,0:T(8,128)(2,1)}, u32[]{:S(2)}) %copy-start) | copy-done | bytes 3686424
  3.5 0.0 copy-start.1
  3.5 0.9 copy-done.1
  4.4 0.0 copy-start.2
  4.4 0.9 copy-done.2
  5.3 0.0 copy-start.3
  5.3 0.7 copy-done.3
  6.0 0.0 copy-start.4
  6.0 0.7 copy-done.4
  6.7 0.0 copy-start.5
  6.7 0.7 copy-done.5
  7.4 0.0 copy-start.6
  7.4 0.7 copy-done.6
  8.0 84.3 %relax.1 = (f32[2,3,8,320]{3,2,1,0:T(8,128)S(1)}, f32[2,3,8,320]{3,2,1,0:T(8,128)S(1)}) custom-call(s32[3,3]{1,0:T(4,128)S(1)} %copy-done.5, s32[4]{0:T(128)S(1)} %copy-done.6, s32[1]{0:T(128)S(6)} %copy.12.pad_ref, f32[2,3,8,320]{3,2,1,0:T(8,128)S(1)} %copy-done.1, f32[2,3,8,320]{3,2,1,0:T(8,128)S(1)} %copy-done.2, ...), custom_call_target="tpu_custom_call" | custom-call | flops 943718400 | bytes 3686400 | tf_op jit(solution)/shard_map/relax/pallas_call | solution.py:308
  92.4 0.6 copy.13
  93.0 0.6 copy.14
Async XLA Ops:
  1.3 2.3 %copy-start = (bf16[2,3,3,320,320]{4,3,2,1,0:T(8,128)(2,1)S(1)}, bf16[2,3,3,320,320]{4,3,2,1,0:T(8,128)(2,1)}, u32[]{:S(2)}) copy-start(bf16[2,3,3,320,320]{4,3,2,1,0:T(8,128)(2,1)} %jac_hbm.1) | copy-start | bytes 11059204
  3.5 0.9 copy-start.1
  4.4 0.9 copy-start.2
  5.3 0.7 copy-start.3
  6.0 0.7 copy-start.4
  6.7 0.7 copy-start.5
  7.4 0.7 copy-start.6

commit v3 on v0

--- a/solution.py
+++ b/solution.py
@@ -29,13 +29,18 @@
     slots_ref,
     halo_ref,
     pad_ref,
+    init_hbm,
+    src_hbm,
+    jac_hbm,
+    vol_hbm,
+    step_hbm,
+    adj_out,
+    res_out,
     init_ref,
     src_in_ref,
     jac_ref,
     vol_ref,
     step_in_ref,
-    adj_out,
-    res_out,
     adj,
     halo_out,
     from_prev,
@@ -53,6 +58,7 @@
     prev_sem,
     next_sem,
     peer_sem,
+    load_sem,
 ):
     rows, width = vol_ref.shape
     reach = from_prev.shape[1]
@@ -65,6 +71,20 @@
     d = lax.axis_index("cell")
     before = lax.rem(d + cells - 1, cells)
     after = lax.rem(d + 1, cells)
+    loads = [
+        pltpu.make_async_copy(hbm, ref, load_sem.at[n])
+        for n, (hbm, ref) in enumerate(
+            (
+                (init_hbm, init_ref),
+                (src_hbm, src_in_ref),
+                (vol_hbm, vol_ref),
+                (step_hbm, step_in_ref),
+                (jac_hbm, jac_ref),
+            )
+        )
+    ]
+    for load in loads:
+        load.start()
     others = [lax.rem(a + m, insts) for m in range(1, insts)]
 
     barrier = pltpu.get_barrier_semaphore()
@@ -78,6 +98,8 @@
             [first[:, :main], first[:, main:], second[:, main:], second[:, :main]], axis=1
         )
 
+    for load in loads[:4]:
+        load.wait()
     for r in range(rows):
         adj[0, r] = pack(init_ref[0, r], init_ref[1, r])
         src[r] = pack(src_in_ref[0, r], src_in_ref[1, r])
@@ -101,12 +123,6 @@
                     [jnp.zeros((hi - lo, 128 - tail), jnp.bfloat16), block[lo:hi, main:]], axis=1
                 )
             dst[: 128 - tail, :] = jnp.zeros((128 - tail, wide), jnp.bfloat16)
-
-    for r in range(rows):
-        for t in range(2):
-            expand(t, r, 0, near.at[r, t])
-            for k in (1, 2):
-                expand(t, r, k, far.at[r, t, (k - 1) * wide : k * wide, :])
 
     def split(x):
         parts = []
@@ -172,6 +188,15 @@
         for copy in copies:
             copy.start()
 
+        @pl.when(s == 0)
+        def _():
+            loads[4].wait()
+            for r in range(rows):
+                for t in range(2):
+                    expand(t, r, 0, near.at[r, t])
+                    for k in (1, 2):
+                        expand(t, r, k, far.at[r, t, (k - 1) * wide : k * wide, :])
+
         for r in range(rows):
             x = split(adj[now, r])
             flux[r] = merge(
@@ -270,9 +295,14 @@
     return pl.pallas_call(
         functools.partial(kernel, insts, cells),
         out_shape=(out, out),
-        in_specs=[smem] * 3 + [vmem] * 5,
+        in_specs=[smem] * 3 + [pl.BlockSpec(memory_space=pltpu.HBM)] * 5,
         out_specs=(vmem, vmem),
         scratch_shapes=[
+            pltpu.VMEM(adjoint_init.shape, f32),
+            pltpu.VMEM(adjoint_init.shape, f32),
+            pltpu.VMEM(jacobian.shape, bf16),
+            pltpu.VMEM(volume.shape, f32),
+            pltpu.VMEM(volume.shape, f32),
             pltpu.VMEM((2, rows) + block, f32),
             pltpu.VMEM((2, 2 * reach) + block, f32),
             pltpu.VMEM((2, reach) + block, f32),
@@ -290,9 +320,10 @@
             pltpu.SemaphoreType.DMA((2,)),
             pltpu.SemaphoreType.DMA((2,)),
             pltpu.SemaphoreType.DMA((2, insts - 1)),
+            pltpu.SemaphoreType.DMA((5,)),
         ],
         compiler_params=pltpu.CompilerParams(
-            collective_id=0, has_side_effects=True, vmem_limit_bytes=40 * 1024 * 1024
+            collective_id=0, has_side_effects=True, vmem_limit_bytes=64 * 1024 * 1024 - 256 * 1024
         ),
         cost_estimate=pl.CostEstimate(
             flops=flops, bytes_accessed=2 * jacobian.size, transcendentals=0

time: 89.2 us -> 85.5 us (0.959)
  local copies, waits for them, and re-layouts: 8 us -> 3.04 us
  Pallas kernels: 79.6 us -> 80.9 us
    unnamed x16 -> x2, local copies, waits for them, and re-layouts: 8 us -> 3.04 us
    pallas_call x1, Pallas kernels: 79.6 us -> 80.9 us  [on_device(): pl.pallas_call(functools.partial(kernel, insts, cells), out_shape=(out, o...]
where the time goes in v3:
time: 85.5 us; the launch traced here: 85.3 us
  Pallas kernels  80.9 us (95%)
  local copies, waits for them, and re-layouts  3.04 us (4%)
  between operations  1.29 us (2%)
    pallas_call x1, Pallas kernels, on_device(): pl.pallas_call(functools.partial(kernel, insts, cells), out_shape=(out, o...  80.9 us
    unnamed x2, local copies, waits for them, and re-layouts  3.04 us

profile of v3, /device:TPU:0, one launch (start us, length us, event | category | flops | bytes accessed | tf_op | source)
XLA Modules:
  0.0 85.3 jit_solution(12589772907076524610)
XLA Ops:
  1.3 80.9 %relax.1 = (f32[2,3,8,320]{3,2,1,0:T(8,128)}, f32[2,3,8,320]{3,2,1,0:T(8,128)}) custom-call(s32[3,3]{1,0:T(4,128)} %slots_ref.1, s32[4]{0:T(128)} %halo_ref.1, s32[1]{0:T(128)S(6)} %copy.12.pad_ref, f32[2,3,8,320]{3,2,1,0:T(8,128)} %init_hbm.1, f32[2,3,8,320]{3,2,1,0:T(8,128)} %src_hbm.1, bf16[2,3,3,320,320]{4,3,2,1,0:T(8,128)(2,1)} %jac_hbm.1, ...), custom_call_target="tpu_custom_call" | custom-call | flops 943718400 | bytes 3686400 | tf_op jit(solution)/shard_map/relax/pallas_call | solution.py:295
  82.2 1.5 %copy.13 = f32[2,3,8,320]{3,2,1,0:T(8,128)} copy(f32[2,3,8,320]{3,2,1,0:T(8,128)} %get-tuple-element.4) | data formatting | bytes 122880
  83.8 1.5 %copy.14 = f32[2,3,8,320]{3,2,1,0:T(8,128)} copy(f32[2,3,8,320]{3,2,1,0:T(8,128)} %get-tuple-element.5) | data formatting | bytes 122880

commit v4 on v3

--- a/solution.py
+++ b/solution.py
@@ -151,11 +151,7 @@
 
     pl.semaphore_wait(barrier, insts + 1)
 
-    def sweep(s, carry):
-        now = lax.rem(s, 2)
-        later = 1 - now
-        for h in range(2 * reach):
-            halo_out[now, h] = adj[now, halo_ref[h]]
+    def exchange(now):
         copies = [
             pltpu.make_async_remote_copy(
                 halo_out.at[now, 0:reach],
@@ -185,6 +181,14 @@
                     device_id_type=MESH,
                 )
             )
+        return copies
+
+    def sweep(s, carry):
+        now = lax.rem(s, 2)
+        later = 1 - now
+        for h in range(2 * reach):
+            halo_out[now, h] = adj[now, halo_ref[h]]
+        copies = exchange(now)
         for copy in copies:
             copy.start()
 
@@ -203,6 +207,11 @@
                 join(jnp.dot(x[:, :wide], near[r, 0], preferred_element_type=jnp.float32)),
                 join(jnp.dot(x[:, packed - wide :], near[r, 1], preferred_element_type=jnp.float32)),
             )
+
+        @pl.when(s > 0)
+        def _():
+            for copy in exchange(later):
+                copy.wait_send()
 
         copies[0].wait_recv()
         for h in range(reach):
@@ -261,11 +270,11 @@
                     out[1, r, :, :main] = value[:, wide:]
                     out[1, r, :, main:] = value[:, width:wide]
 
-        for copy in copies:
-            copy.wait_send()
         return carry
 
     lax.fori_loop(0, ITERS, sweep, 0)
+    for copy in exchange((ITERS - 1) % 2):
+        copy.wait_send()
 
 
 def on_device(
@@ -323,7 +332,7 @@
             pltpu.SemaphoreType.DMA((5,)),
         ],
         compiler_params=pltpu.CompilerParams(
-            collective_id=0, has_side_effects=True, vmem_limit_bytes=64 * 1024 * 1024 - 256 * 1024
+            collective_id=0, has_side_effects=True, vmem_limit_bytes=64 * 1024 * 1024 - 512 * 1024
         ),
         cost_estimate=pl.CostEstimate(
             flops=flops, bytes_accessed=2 * jacobian.size, transcendentals=0

time: 85.5 us -> 85.4 us (level)
  no operation moved by 1% of the time
where the time goes in v4:
time: 85.4 us; the launch traced here: 85.2 us
  Pallas kernels  80.8 us (95%)
  local copies, waits for them, and re-layouts  3.04 us (4%)
  between operations  1.29 us (2%)
    pallas_call x1, Pallas kernels, on_device(): pl.pallas_call(functools.partial(kernel, insts, cells), out_shape=(out, o...  80.8 us
    unnamed x2, local copies, waits for them, and re-layouts  3.04 us

profile of v4, /device:TPU:0, one launch (start us, length us, event | category | flops | bytes accessed | tf_op | source)
XLA Modules:
  0.0 85.2 jit_solution(9525479840755884690)
XLA Ops:
  1.3 80.8 %relax.1 = (f32[2,3,8,320]{3,2,1,0:T(8,128)}, f32[2,3,8,320]{3,2,1,0:T(8,128)}) custom-call(s32[3,3]{1,0:T(4,128)} %slots_ref.1, s32[4]{0:T(128)} %halo_ref.1, s32[1]{0:T(128)S(6)} %copy.12.pad_ref, f32[2,3,8,320]{3,2,1,0:T(8,128)} %init_hbm.1, f32[2,3,8,320]{3,2,1,0:T(8,128)} %src_hbm.1, bf16[2,3,3,320,320]{4,3,2,1,0:T(8,128)(2,1)} %jac_hbm.1, ...), custom_call_target="tpu_custom_call" | custom-call | flops 943718400 | bytes 3686400 | tf_op jit(solution)/shard_map/relax/pallas_call | solution.py:304
  82.1 1.5 %copy.13 = f32[2,3,8,320]{3,2,1,0:T(8,128)} copy(f32[2,3,8,320]{3,2,1,0:T(8,128)} %get-tuple-element.4) | data formatting | bytes 122880
  83.6 1.5 %copy.14 = f32[2,3,8,320]{3,2,1,0:T(8,128)} copy(f32[2,3,8,320]{3,2,1,0:T(8,128)} %get-tuple-element.5) | data formatting | bytes 122880
